TPU v7x, 32 devices: a whole 2x2x4 slice. The times are simulated.
32 devices in a mesh: req: 8 (over z, x), tp: 4 (over y, core).
Axes of the slice: x: 2, y: 2, z: 4, core: 2. Of those that a mesh axis runs over, the one named last changes fastest.
Arguments:
- layer_in: bfloat16 [4, 64, 2880], P(None, 'req'), may hold values from -3 to 3
- query_in: bfloat16 [4, 64, 2048], P(None, 'req', 'tp'), may hold values from -6 to 6
- unrotated_key: bfloat16 [4, 64, 512], P(None, 'req', 'tp'), may hold values from -6 to 6
- incoming_value: bfloat16 [4, 64, 512], P(None, 'req', 'tp'), may hold values from -12 to 12
- rotated_prompt_keys: bfloat16 [64, 256, 512], P('req', None, 'tp'), may hold values from -270 to 270
- prompt_value_rows: bfloat16 [64, 256, 512], P('req', None, 'tp'), may hold values from -6 to 6
- generated_key_rows: bfloat16 [64, 64, 512], P('req', None, 'tp'), may hold values from -9 to 9
- generated_value_rows: bfloat16 [64, 64, 512], P('req', None, 'tp'), may hold values from -12 to 12
- lengths: int32 [8], replicated, may hold values from 128 to 2048, as said below
- parents: int32 [4, 8, 8], replicated, may hold values from 0 to 7
- routes: int32 [4, 64, 4], P(None, 'req'), may hold values from 0 to 15, all different within a row; in each aligned block of 8 rows (0 to 7, 8 to 15, ..., all dimensions but the last counted through in order) at most 4 rows name the same one
- head_sink_logits: float32 [32], P('tp'), may hold values from 1 to 6
- out_weight: bfloat16 [2048, 2880], P('tp'), may hold values from -0.5 to 0.5
- mlp_gain: float32 [2880], replicated, may hold values from 0.5 to 1.5
- router_weight: bfloat16 [2880, 16], replicated, may hold values from -0.21875 to 0.21875
- expert_gate: bfloat16 [16, 2880, 2880], P('req', None, 'tp'), may hold values from -0.4375 to 0.4375
- expert_up: bfloat16 [16, 2880, 2880], P('req', None, 'tp'), may hold values from -0.4375 to 0.4375
- expert_down: bfloat16 [16, 2880, 2880], P('req', 'tp'), may hold values from -0.109375 to 0.109375
- next_gain: float32 [2880], replicated, may hold values from 0.5 to 1.5
- next_q_weight: bfloat16 [2880, 2048], P(None, 'tp'), may hold values from -0.109375 to 0.109375
- following_key_value_weight: bfloat16 [2880, 2, 512], P(None, None, 'tp'), may hold values from -0.109375 to 0.109375
Outputs:
- layer_out: bfloat16 [4, 64, 2880], P(None, 'req')
- next_query: bfloat16 [4, 64, 2048], P(None, 'req', 'tp')
- next_keyval: bfloat16 [4, 64, 2, 512], P(None, 'req', None, 'tp')
Inputs may be any that keep to these rules, and one draw needn't show every extreme that they name: `lengths`: some group's prompt holds exactly 2048 positions. `routes`: a row names 4 different experts; in the rows of one device at one step no expert is named more than 4 times, a bound that some block reaches.
All inputs are finite; a program needn't handle non-finite values.
Results may differ from a plain program's by a relative error of at most 0.029.
Values may be sent and summed in bfloat16 or wider, within the bound.
A program may use at most 128 MiB of HBM per device.

v0:
```python
import jax
import jax.numpy as jnp
from jax import lax
from jax.sharding import PartitionSpec as P

HEAD = 64
EXPERTS = 16
THETA = 150000.0
EPS = 1e-05
NEG = -1e30
BF = jnp.bfloat16
F32 = jnp.float32


def rope(vectors, positions):
    half = HEAD // 2
    powers = jnp.arange(half, dtype=F32) * (2.0 / HEAD)
    angles = positions.astype(F32)[..., None, None] * jnp.power(THETA, -powers)
    cos, sin = (jnp.cos(angles), jnp.sin(angles))
    lower, upper = (vectors[..., :half], vectors[..., half:])
    return jnp.concatenate([lower * cos - upper * sin, lower * sin + upper * cos], axis=-1)


def rms(rows, gain):
    return rows * lax.rsqrt(jnp.mean(rows * rows, axis=-1, keepdims=True) + EPS) * gain


def lineage_tables(parents):
    steps, groups, beams = parents.shape
    ident = jnp.broadcast_to(jnp.arange(beams, dtype=jnp.int32), (groups, beams))
    first = []
    tokens = [[None] * steps for _ in range(steps)]
    for t in range(steps):
        walker = ident
        for s in range(t, -1, -1):
            tokens[s][t] = walker
            hot = walker[..., None] == jnp.arange(beams, dtype=jnp.int32)
            walker = jnp.sum(jnp.where(hot, parents[s][:, None, :], 0), axis=-1)
        first.append(walker)
        for s in range(t + 1, steps):
            tokens[s][t] = jnp.full_like(ident, -1)
    return (jnp.stack(first), jnp.stack([jnp.stack(row) for row in tokens]))


def local(
    layer_in,
    query_in,
    key_in,
    value_in,
    prompt_keys,
    prompt_values,
    gen_keys,
    gen_values,
    lengths,
    parents,
    routes,
    sinks,
    out_weight,
    mlp_gain,
    router_weight,
    expert_gate,
    expert_up,
    expert_down,
    next_gain,
    next_q_weight,
    next_kv_weight,
):
    req_count = lax.axis_size("req")
    me = lax.axis_index("req")
    T, B, q_width = query_in.shape
    kv_width = key_in.shape[2]
    K = kv_width // HEAD
    R = q_width // kv_width
    J = parents.shape[2]
    span = req_count // J
    beam = me // span
    start = me % span * B
    groups = [[c + span * j for j in range(J)] for c in range(span)]
    if span == 1:
        groups = None
    lens = lax.dynamic_slice_in_dim(lengths, start, B)
    pars = lax.dynamic_slice_in_dim(parents, start, B, axis=1)
    S = prompt_keys.shape[1]
    G = gen_keys.shape[1]
    pos = lens[None, :] + G + jnp.arange(T, dtype=jnp.int32)[:, None]
    q = rope(query_in.astype(F32).reshape(T, B, K * R, HEAD), pos).astype(BF).reshape(T, B, q_width)
    k = rope(key_in.astype(F32).reshape(T, B, K, HEAD), pos).astype(BF).reshape(T, B, kv_width)
    q_all = lax.all_gather(q, "req", axis_index_groups=groups)
    first, tokens = lineage_tables(pars)
    prompt_ok = (beam * S + jnp.arange(S, dtype=jnp.int32))[None, :] < lens[:, None]
    mask = jnp.concatenate(
        [
            jnp.broadcast_to(prompt_ok[:, None, None, :], (B, J, T, S)),
            jnp.broadcast_to((first == beam).transpose(1, 2, 0)[..., None], (B, J, T, G)),
            (tokens == beam).transpose(2, 3, 1, 0),
        ],
        axis=-1,
    )
    keys = jnp.concatenate([prompt_keys, gen_keys, k.transpose(1, 0, 2)], axis=1)
    values = jnp.concatenate([prompt_values, gen_values, value_in.transpose(1, 0, 2)], axis=1)
    keys = keys.reshape(B, S + G + T, K, HEAD)
    values = values.reshape(B, S + G + T, K, HEAD)
    qs = q_all.reshape(J, T, B, K, R, HEAD)
    scores = jnp.einsum("jtbkrd,bskd->bkjtrs", qs, keys, preferred_element_type=F32) * 0.125
    usable = mask[:, None, :, :, None, :]
    scores = jnp.where(usable, scores, NEG)
    high = jnp.max(scores, axis=-1)
    weights = jnp.where(usable, jnp.exp(scores - high[..., None]), 0.0)
    total = jnp.sum(weights, axis=-1)
    part = jnp.einsum("bkjtrs,bskd->jtbkrd", weights.astype(BF), values, preferred_element_type=F32)
    high = high.transpose(2, 3, 0, 1, 4)
    total = total.transpose(2, 3, 0, 1, 4)
    part = (part / jnp.maximum(total, 1e-30)[..., None]).astype(BF)
    stats = jnp.stack([high, total], axis=1)
    part = lax.all_to_all(part, "req", 0, 0, axis_index_groups=groups)
    stats = lax.all_to_all(stats, "req", 0, 0, axis_index_groups=groups)
    high, total = (stats[:, 0], stats[:, 1])
    sink = sinks.reshape(K, R)
    peak = jnp.maximum(jnp.max(high, axis=0), sink)
    share = total * jnp.exp(high - peak)
    bottom = jnp.sum(share, axis=0) + jnp.exp(sink - peak)
    attended = jnp.sum(part.astype(F32) * (share / bottom)[..., None], axis=0)
    attended = attended.astype(BF).reshape(T * B, q_width)
    projected = jnp.dot(attended, out_weight, preferred_element_type=F32)
    x1 = layer_in.reshape(T * B, -1).astype(F32) + lax.psum(projected.astype(BF), "tp").astype(F32)
    h2 = rms(x1, mlp_gain).astype(BF)
    logits = jnp.dot(h2, router_weight, preferred_element_type=F32)
    hot = jnp.sum(
        (routes.reshape(T * B, -1, 1) == jnp.arange(EXPERTS, dtype=jnp.int32)).astype(F32), axis=1
    )
    masked = jnp.where(hot > 0, logits, NEG)
    raw = jnp.where(hot > 0, jnp.exp(masked - jnp.max(masked, axis=-1, keepdims=True)), 0.0)
    gates = raw / jnp.sum(raw, axis=-1, keepdims=True)
    h2_all = lax.all_gather(h2, "req", tiled=True)
    gates_all = lax.all_gather(gates, "req", tiled=True)
    slabs = expert_gate.shape[0]
    split = slabs * req_count // EXPERTS
    moe = 0.0
    for s in range(slabs):
        expert = (me * slabs + s) // split
        weight = lax.dynamic_slice_in_dim(gates_all, expert, 1, axis=1)
        gate = jnp.minimum(jnp.dot(h2_all, expert_gate[s], preferred_element_type=F32), 7.0)
        up = jnp.clip(jnp.dot(h2_all, expert_up[s], preferred_element_type=F32), -7.0, 7.0)
        hidden = ((up + 1.0) * gate * jax.nn.sigmoid(1.702 * gate) * weight).astype(BF)
        moe = moe + jnp.dot(hidden, expert_down[s], preferred_element_type=F32)
    moe = lax.psum_scatter(moe.astype(BF), "req", scatter_dimension=0, tiled=True)
    moe = lax.psum(moe, "tp").astype(F32)
    x2 = x1 + moe
    h3 = rms(x2, next_gain).astype(BF)
    next_query = jnp.dot(h3, next_q_weight, preferred_element_type=F32).astype(BF)
    next_kv = jnp.einsum("nd,dcf->ncf", h3, next_kv_weight, preferred_element_type=F32).astype(BF)
    return (
        x2.astype(BF).reshape(T, B, -1),
        next_query.reshape(T, B, q_width),
        next_kv.reshape(T, B, 2, kv_width),
    )


def solution(mesh):
    placed = (
        P(None, "req", None),
        P(None, "req", "tp"),
        P(None, "req", "tp"),
        P(None, "req", "tp"),
        P("req", None, "tp"),
        P("req", None, "tp"),
        P("req", None, "tp"),
        P("req", None, "tp"),
        P(),
        P(),
        P(None, "req", None),
        P("tp"),
        P("tp", None),
        P(),
        P(),
        P("req", None, "tp"),
        P("req", None, "tp"),
        P("req", "tp", None),
        P(),
        P(None, "tp"),
        P(None, None, "tp"),
    )
    return jax.shard_map(
        local,
        mesh=mesh,
        in_specs=placed,
        out_specs=(P(None, "req", None), P(None, "req", "tp"), P(None, "req", None, "tp")),
        check_vma=False,
    )
```

profile of v0, /device:TPU:0, one launch (start us, length us, event | category | flops | bytes accessed | tf_op | source)
XLA Modules:
  0.0 316.0 jit_solution(11140793845565401066)
XLA Ops:
  14.3 34.5 %all_gather.9 = bf16[8,4,8,512]{3,2,1,0:T(8,128)(2,1)} all-gather(bf16[1,4,8,512]{3,2,1,0:T(8,128)(2,1)S(1)} %convert_element_type.87), channel_id=1, replica_groups=mesh['req'=8,'tp'=4] {'req'}, dimensions={0}, use_global_device_ids=true | all-gather | bytes 294912 | tf_op jit(solution)/shard_map/all_gather | solution.py:88
  50.1 2.0 pad_maximum_fusion.1
  52.1 2.2 copy.122
  54.6 2.0 fusion.24
  62.6 5.5 %all-to-all-start.1 = ((f32[8,1,512]{2,1,0:T(1,128)}), f32[8,1,512]{2,1,0:T(1,128)S(1)}, u32[]{:S(2)}, u32[]{:S(2)}) async-start(f32[8,1,512]{2,1,0:T(1,128)} %reshape.201), calls=%async_computation.1 | async-start | bytes 32768 | tf_op jit(solution)/shard_map/all_to_all | solution.py:116
  68.1 2.0 pad_maximum_fusion
  70.1 2.2 copy.115
  72.4 3.9 %divide_convert_fusion = bf16[8,4,8,2,4,64]{5,0,4,1,3,2:T(8,128)(2,1)} fusion(bf16[8,324,2,64,1,1]{1,3,5,4,2,0:T(8,128)(2,1)} %bitcast.191, f32[8,2,8,4,4,324]{5,2,4,3,1,0:T(8,128)} %copy-done.1, f32[8,2,8,4,4]{2,4,3,1,0:T(4,128)S(1)} %copy-done.6, pred[8,8,4,324]{3,1,2,0:T(8,128)(4,1)} %copy-done.7, f32[8,4,8,2,4]{0,4,1,3,2:T(4,128)S(1)} %bitcast_maximum_fusion), kind=kOutput, calls=%fused_computation.55 | convolution fusion | flops 88514560 | bytes 3679232 | tf_op jit(solution)/shard_map/bkjtrs,bskd->jtbkrd/dot_general | solution.py:110
  78.7 6.0 %all-to-all-start = ((bf16[8,2,8192]{2,1,0:T(2,128)(2,1)}), bf16[8,2,8192]{2,1,0:T(2,128)(2,1)}, u32[]{:S(2)}, u32[]{:S(2)}) async-start(bf16[8,2,8192]{2,1,0:T(2,128)(2,1)} %reshape.199), calls=%async_computation | async-start | bytes 524288 | tf_op jit(solution)/shard_map/all_to_all | solution.py:115
  87.1 5.9 %all-to-all-done = bf16[8,2,8192]{2,1,0:T(2,128)(2,1)} async-done(((bf16[8,2,8192]{2,1,0:T(2,128)(2,1)}), bf16[8,2,8192]{2,1,0:T(2,128)(2,1)}, u32[]{:S(2)}, u32[]{:S(2)}) %all-to-all-start) | async-done | bytes 262176 | tf_op jit(solution)/shard_map/all_to_all | solution.py:115
  93.0 2.1 reshape.200
  95.1 1.7 multiply_reduce_fusion
  98.7 29.9 %all-reduce.3.cloned.1.call-done = bf16[32,2880]{1,0:T(8,128)(2,1)} async-done(((bf16[32,2880]{1,0:T(8,128)(2,1)}), bf16[32,2880]{1,0:T(8,128)(2,1)}) %all-reduce.3.cloned.1.call-update) | async-done | bytes 184336 | tf_op jit(solution)/shard_map/psum | solution.py:125
  129.8 1.7 multiply_convert_fusion.1
  132.8 30.8 %all-gather = f32[8,32,16]{1,2,0:T(8,128)S(1)} all-gather(f32[1,32,16]{1,2,0:T(8,128)S(1)} %divide_bitcast_fusion), channel_id=1, replica_groups=mesh['req'=8,'tp'=4] {'req'}, dimensions={0}, use_global_device_ids=true | all-gather | bytes 18432 | tf_op jit(solution)/shard_map/all_gather | solution.py:135
  163.8 11.5 %all-gather.3.cloned.1.call-done = bf16[256,2880]{1,0:T(8,128)(2,1)} async-done(((bf16[32,2880]{1,0:T(8,128)(2,1)}), bf16[256,2880]{1,0:T(8,128)(2,1)}) %all-gather.3.cloned.1.call-update) | async-done | bytes 1474576 | tf_op jit(solution)/shard_map/all_gather | solution.py:134
  175.3 5.0 %fusion.48 = f32[256,720]{0,1:T(8,128)} fusion(bf16[256,2880]{1,0:T(8,128)(2,1)} %all-gather.3.cloned.1.call-done, bf16[2,2880,720]{1,2,0:T(8,128)(2,1)} %param.36), kind=kOutput, calls=%fused_computation.38 | convolution fusion | flops 1061867520 | bytes 6483968 | tf_op jit(solution)/shard_map/dot_general | solution.py:142
  180.3 4.4 %fusion.42 = f32[256,720]{0,1:T(8,128)} fusion(bf16[256,2880]{1,0:T(8,128)(2,1)S(1)} %copy-done.13, bf16[2,2880,720]{1,2,0:T(8,128)(2,1)} %param.36), kind=kOutput, calls=%fused_computation.36 | convolution fusion | flops 1061867520 | bytes 6451200 | tf_op jit(solution)/shard_map/dot_general | solution.py:142
  184.7 10.7 %fusion = f32[256,2880]{1,0:T(8,128)} fusion(bf16[2,720,2880]{2,1,0:T(8,128)(2,1)} %param.38, f32[256,720]{0,1:T(8,128)} %fusion.48, bf16[256,2880]{1,0:T(8,128)(2,1)} %all-gather.3.cloned.1.call-done, bf16[2,2880,720]{1,2,0:T(8,128)(2,1)} %param.37, f32[256]{0:T(256)S(1)} %bitcast.205), kind=kOutput, calls=%fused_computation | convolution fusion | flops 2125209600 | bytes 13673472 | tf_op jit(solution)/shard_map/dot_general | solution.py:145
  195.3 11.1 %fusion.21 = bf16[256,2880]{1,0:T(8,128)(2,1)} fusion(f32[256,2880]{1,0:T(8,128)} %fusion, bf16[2,720,2880]{2,1,0:T(8,128)(2,1)} %param.38, f32[256,720]{0,1:T(8,128)} %fusion.42, bf16[256,2880]{1,0:T(8,128)(2,1)} %all-gather.3.cloned.1.call-done, bf16[2,2880,720]{1,2,0:T(8,128)(2,1)} %param.37, f32[256]{0:T(256)S(1)} %bitcast.204), kind=kOutput, calls=%fused_computation.19 | convolution fusion | flops 2126684160 | bytes 15213568 | tf_op jit(solution)/shard_map/dot_general | solution.py:145
  206.5 63.7 %reduce-scatter.2.cloned.1.call-done = bf16[32,2880]{1,0:T(8,128)(2,1)} async-done(((bf16[256,2880]{1,0:T(8,128)(2,1)}), bf16[32,2880]{1,0:T(8,128)(2,1)}) %reduce-scatter.2.cloned.1.call-update) | async-done | bytes 184336 | tf_op jit(solution)/shard_map/reduce_scatter | solution.py:146
  270.2 32.6 %all-reduce.5.cloned.1.call-done = bf16[32,2880]{1,0:T(8,128)(2,1)} async-done(((bf16[32,2880]{1,0:T(8,128)(2,1)}), bf16[32,2880]{1,0:T(8,128)(2,1)}) %all-reduce.5.cloned.1.call-update) | async-done | bytes 184336 | tf_op jit(solution)/shard_map/psum | solution.py:147
  304.2 1.7 multiply_convert_fusion
  305.9 1.7 fusion.85
  (112 shorter events, 26.8 us)
Async XLA Ops:
  7.2 89.8 %copy-start = (bf16[512,2880]{0,1:T(8,128)(2,1)S(1)}, bf16[512,2880]{0,1:T(8,128)(2,1)}, u32[]{:S(2)}) copy-start(bf16[512,2880]{0,1:T(8,128)(2,1)} %param.33) | copy-start | bytes 8847364
  54.6 5.0 %copy-start.7 = (pred[8,8,4,324]{3,1,2,0:T(8,128)(4,1)}, pred[8,8,4,324]{3,1,2,0:T(8,128)(4,1)S(1)}, u32[]{:S(2)}) copy-start(pred[8,8,4,324]{3,1,2,0:T(8,128)(4,1)S(1)} %pad_add_fusion) | copy-start | bytes 248836
  56.7 1.7 copy-start.1
  56.7 2.9 copy-start.5
  56.7 11.4 %copy-start.11 = (bf16[4,8,128]{2,1,0:T(8,128)(2,1)S(1)}, bf16[4,8,128]{2,1,0:T(8,128)(2,1)}, u32[]{:S(2)}) copy-start(bf16[4,8,128]{2,1,0:T(8,128)(2,1)} %param.24) | copy-start | bytes 24580
  60.4 12.0 %copy-start.6 = (f32[8,2,8,4,4]{2,4,3,1,0:T(4,128)S(1)}, f32[8,2,8,4,4]{2,4,3,1,0:T(4,128)}, u32[]{:S(2)}) copy-start(f32[8,2,8,4,4]{2,4,3,1,0:T(4,128)} %copy-done.5) | copy-start | bytes 24580
  62.6 16.1 %all-to-all-start.1 = ((f32[8,1,512]{2,1,0:T(1,128)}), f32[8,1,512]{2,1,0:T(1,128)S(1)}, u32[]{:S(2)}, u32[]{:S(2)}) async-start(f32[8,1,512]{2,1,0:T(1,128)} %reshape.201), calls=%async_computation.1 | async-start | bytes 32768 | tf_op jit(solution)/shard_map/all_to_all | solution.py:116
  72.4 3.9 %copy-start.14 = (f32[8]{0:T(128)S(1)}, f32[8]{0:T(128)}, u32[]{:S(2)}) copy-start(f32[8]{0:T(128)} %param.32) | copy-start | bytes 100
  78.7 14.3 %all-to-all-start = ((bf16[8,2,8192]{2,1,0:T(2,128)(2,1)}), bf16[8,2,8192]{2,1,0:T(2,128)(2,1)}, u32[]{:S(2)}, u32[]{:S(2)}) async-start(bf16[8,2,8192]{2,1,0:T(2,128)(2,1)} %reshape.199), calls=%async_computation | async-start | bytes 524288 | tf_op jit(solution)/shard_map/all_to_all | solution.py:115
  84.7 44.0 %all-reduce.3.cloned.1.call-start = ((), (), s32[]{:S(2)}) async-start(), calls=%async_computation.3 | async-start | bytes 376832 | tf_op jit(solution)/shard_map/psum | solution.py:125
  86.4 42.3 %copy-start.2 = (bf16[4,8,2880]{2,1,0:T(8,128)(2,1)S(1)}, bf16[4,8,2880]{2,1,0:T(8,128)(2,1)}, u32[]{:S(2)}) copy-start(bf16[4,8,2880]{2,1,0:T(8,128)(2,1)} %param.21) | copy-start | bytes 552964
  86.6 43.2 %copy-start.10 = (f32[2880]{0:T(1024)S(1)}, f32[2880]{0:T(1024)}, u32[]{:S(2)}) copy-start(f32[2880]{0:T(1024)} %param.34) | copy-start | bytes 34564
  87.1 44.5 %copy-start.12 = (s32[4,8,4]{1,2,0:T(4,128)S(1)}, s32[4,8,4]{1,2,0:T(4,128)}, u32[]{:S(2)}) copy-start(s32[4,8,4]{1,2,0:T(4,128)} %param.31) | copy-start | bytes 1540
  87.1 44.6 %copy-start.8 = (bf16[2880,16]{0,1:T(8,128)(2,1)S(1)}, bf16[2880,16]{0,1:T(8,128)(2,1)}, u32[]{:S(2)}) copy-start(bf16[2880,16]{0,1:T(8,128)(2,1)} %param.35) | copy-start | bytes 276484
  98.6 76.6 %all-gather.3.cloned.1.call-start = ((), (), s32[]{:S(2)}) async-start(), calls=%async_computation.4 | async-start | bytes 1695744 | tf_op jit(solution)/shard_map/all_gather | solution.py:134
  131.5 138.7 %reduce-scatter.2.cloned.1.call-start = ((), (), s32[]{:S(2)}) async-start(), calls=%async_computation.5 | async-start | bytes 1695744 | tf_op jit(solution)/shard_map/reduce_scatter | solution.py:146
  175.3 5.0 %copy-start.13 = (bf16[256,2880]{1,0:T(8,128)(2,1)S(1)}, bf16[256,2880]{1,0:T(8,128)(2,1)}, u32[]{:S(2)}) copy-start(bf16[256,2880]{1,0:T(8,128)(2,1)} %all-gather.3.cloned.1.call-done) | copy-start | bytes 4423684
  195.3 107.5 %copy-start.3 = (bf16[32,2880]{1,0:T(8,128)(2,1)S(1)}, bf16[32,2880]{1,0:T(8,128)(2,1)}, u32[]{:S(2)}) copy-start(bf16[32,2880]{1,0:T(8,128)(2,1)} %all-reduce.3.cloned.1.call-done) | copy-start | bytes 552964
  195.3 108.8 %copy-start.9 = (f32[2880]{0:T(1024)S(1)}, f32[2880]{0:T(1024)}, u32[]{:S(2)}) copy-start(f32[2880]{0:T(1024)} %param.39) | copy-start | bytes 34564
  206.4 96.4 %all-reduce.5.cloned.1.call-start = ((), (), s32[]{:S(2)}) async-start(), calls=%async_computation.6 | async-start | bytes 376832 | tf_op jit(solution)/shard_map/psum | solution.py:147
  302.9 4.8 %copy-start.4 = (bf16[2880,512]{1,0:T(8,128)(2,1)S(1)}, bf16[2880,512]{1,0:T(8,128)(2,1)}, u32[]{:S(2)}) copy-start(bf16[2880,512]{1,0:T(8,128)(2,1)} %param.40) | copy-start | bytes 8847364
Sparse Core Ops, SparseCore 0:
  98.8 29.8 all-reduce.2
  131.6 43.5 all-gather.2
  206.6 63.5 reduce-scatter.1
  272.4 30.4 all-reduce.4
where the time goes:
time: 317 us; the launch traced here: 316 us
  waiting for transfers between devices  144 us (45%)
  blocking collectives  65.4 us (21%)
  matrix products  42.8 us (14%)
  local copies, waits for them, and re-layouts  19.6 us (6%)
  other arithmetic  18.8 us (6%)
  between operations  14.2 us (4%)
  starting transfers between devices  11.6 us (4%)
    reduce_scatter x1, waiting for transfers between devices, local(): lax.psum_scatter(moe.astype(BF), 'req', scatter_dimension=0, tiled=True)  63.7 us
    all_gather x1, blocking collectives, local(): q_all = lax.all_gather(q, 'req', axis_index_groups=groups)  34.5 us
    psum x1, waiting for transfers between devices, local(): moe = lax.psum(moe, 'tp').astype(F32)  32.6 us
    all_gather x1, blocking collectives, local(): gates_all = lax.all_gather(gates, 'req', tiled=True)  30.8 us
    psum x1, waiting for transfers between devices, local(): lax.psum(projected.astype(BF), 'tp').astype(F32)  29.9 us
    dot_general x2, matrix products, local(): moe = moe + jnp.dot(hidden, expert_down[s], preferred_element_type=F32)  21.7 us
    all_gather x1, waiting for transfers between devices, local(): h2_all = lax.all_gather(h2, 'req', tiled=True)  11.5 us
    dot_general x2, matrix products, local(): jnp.dot(h2_all, expert_gate[s], preferred_element_type=F32)  9.4 us
  transfers between devices with their start and end apart: 6, of which 5 were waited for; matrix products, arithmetic and copies ran while one was open for 5% of the time, Pallas kernels for 0%

commit v1 on v0

--- a/solution.py
+++ b/solution.py
@@ -10,6 +10,28 @@
 NEG = -1e30
 BF = jnp.bfloat16
 F32 = jnp.float32
+
+
+def laid_out(blocks, dim):
+    blocks = jnp.moveaxis(blocks, 0, dim)
+    dims = blocks.shape
+    return blocks.reshape(*dims[:dim], dims[dim] * dims[dim + 1], *dims[dim + 2 :])
+
+
+def ring_gather(value, axis, dim):
+    length = lax.axis_size(axis)
+    pairs = [(i, (i + 1) % length) for i in range(length)]
+    back = [(b, a) for a, b in pairs]
+    lower, upper = ([], [])
+    for hop in range(length - 1):
+        if hop % 2 == 0:
+            lower.append(lax.ppermute(lower[-1] if lower else value, axis, pairs))
+        else:
+            upper.append(lax.ppermute(upper[-1] if upper else value, axis, back))
+    blocks = jnp.stack([*lower[::-1], value, *upper])
+    shift = lax.axis_index(axis) - len(lower)
+    blocks = blocks[(jnp.arange(length) - shift) % length]
+    return laid_out(blocks, dim)
 
 
 def rope(vectors, positions):
@@ -132,7 +154,7 @@
     raw = jnp.where(hot > 0, jnp.exp(masked - jnp.max(masked, axis=-1, keepdims=True)), 0.0)
     gates = raw / jnp.sum(raw, axis=-1, keepdims=True)
     h2_all = lax.all_gather(h2, "req", tiled=True)
-    gates_all = lax.all_gather(gates, "req", tiled=True)
+    gates_all = ring_gather(gates, "req", 0)
     slabs = expert_gate.shape[0]
     split = slabs * req_count // EXPERTS
     moe = 0.0

time: 317 us -> 317 us (level)
  blocking collectives: 65.4 us -> 34.5 us
  starting transfers between devices: 11.6 us -> 27.6 us
  waiting for transfers between devices: 144 us -> 158 us
    all_gather x1 -> x0, blocking collectives: 30.8 us -> none  [local(): gates_all = lax.all_gather(gates, 'req', tiled=True)]
    ppermute x0 -> x7, starting transfers between devices: none -> 16 us  [the longest x3 14.4 us: ring_gather(): upper.append(lax.ppermute(upper[-1] if upper else value, axis, back))]
    ppermute x0 -> x7, waiting for transfers between devices: none -> 9.54 us  [the longest x4 9.53 us: ring_gather(): lower.append(lax.ppermute(lower[-1] if lower else value, axis, pairs))]
    all_gather x1, waiting for transfers between devices: 11.5 us -> 16.4 us  [local(): h2_all = lax.all_gather(h2, 'req', tiled=True)]
    unnamed x38 -> x44, local copies, waits for them, and re-layouts: 6.82 us -> 6.76 us
  transfers between devices with their start and end apart: 6 -> 13, of which waited for: 5 -> 9; matrix products, arithmetic and copies ran while one was open for 5% -> 5% of each run, Pallas kernels for 0% -> 0%
where the time goes in v1:
time: 317 us; the launch traced here: 316 us
  waiting for transfers between devices  158 us (50%)
  matrix products  42.8 us (14%)
  blocking collectives  34.5 us (11%)
  starting transfers between devices  27.6 us (9%)
  local copies, waits for them, and re-layouts  20.1 us (6%)
  other arithmetic  18.8 us (6%)
  between operations  14.3 us (5%)
    reduce_scatter x1, waiting for transfers between devices, local(): lax.psum_scatter(moe.astype(BF), 'req', scatter_dimension=0, tiled=True)  63.6 us
    all_gather x1, blocking collectives, local(): q_all = lax.all_gather(q, 'req', axis_index_groups=groups)  34.5 us
    psum x1, waiting for transfers between devices, local(): moe = lax.psum(moe, 'tp').astype(F32)  32.7 us
    psum x1, waiting for transfers between devices, local(): lax.psum(projected.astype(BF), 'tp').astype(F32)  29.9 us
    dot_general x2, matrix products, local(): moe = moe + jnp.dot(hidden, expert_down[s], preferred_element_type=F32)  21.7 us
    all_gather x1, waiting for transfers between devices, local(): h2_all = lax.all_gather(h2, 'req', tiled=True)  16.4 us
    ppermute x3, starting transfers between devices, ring_gather(): upper.append(lax.ppermute(upper[-1] if upper else value, axis, back))  14.4 us
    ppermute x4, waiting for transfers between devices, ring_gather(): lower.append(lax.ppermute(lower[-1] if lower else value, axis, pairs))  9.53 us
  transfers between devices with their start and end apart: 13, of which 9 were waited for; matrix products, arithmetic and copies ran while one was open for 5% of the time, Pallas kernels for 0%

profile of v1, /device:TPU:0, one launch (start us, length us, event | category | flops | bytes accessed | tf_op | source)
XLA Modules:
  0.0 316.2 jit_solution(2496233003103804721)
XLA Ops:
  14.3 34.5 %all_gather.6 = bf16[8,4,8,512]{3,2,1,0:T(8,128)(2,1)} all-gather(bf16[1,4,8,512]{3,2,1,0:T(8,128)(2,1)S(1)} %convert_element_type.87), channel_id=1, replica_groups=mesh['req'=8,'tp'=4] {'req'}, dimensions={0}, use_global_device_ids=true | all-gather | bytes 294912 | tf_op jit(solution)/shard_map/all_gather | solution.py:110
  50.1 2.0 pad_maximum_fusion.1
  52.1 2.2 copy.122
  54.6 2.0 fusion.24
  62.6 5.5 %all-to-all-start.1 = ((f32[8,1,512]{2,1,0:T(1,128)}), f32[8,1,512]{2,1,0:T(1,128)S(1)}, u32[]{:S(2)}, u32[]{:S(2)}) async-start(f32[8,1,512]{2,1,0:T(1,128)} %reshape.260), calls=%async_computation.1 | async-start | bytes 32768 | tf_op jit(solution)/shard_map/all_to_all | solution.py:138
  68.1 2.0 pad_maximum_fusion
  70.1 2.2 copy.115
  72.4 3.9 %divide_convert_fusion = bf16[8,4,8,2,4,64]{5,0,4,1,3,2:T(8,128)(2,1)} fusion(bf16[8,324,2,64,1,1]{1,3,5,4,2,0:T(8,128)(2,1)} %bitcast.207, f32[8,2,8,4,4,324]{5,2,4,3,1,0:T(8,128)} %copy-done.1, f32[8,2,8,4,4]{2,4,3,1,0:T(4,128)S(1)} %copy-done.6, pred[8,8,4,324]{3,1,2,0:T(8,128)(4,1)} %copy-done.7, f32[8,4,8,2,4]{0,4,1,3,2:T(4,128)S(1)} %bitcast_maximum_fusion), kind=kOutput, calls=%fused_computation.56 | convolution fusion | flops 88514560 | bytes 3679232 | tf_op jit(solution)/shard_map/bkjtrs,bskd->jtbkrd/dot_general | solution.py:132
  78.8 6.0 %all-to-all-start = ((bf16[8,2,8192]{2,1,0:T(2,128)(2,1)}), bf16[8,2,8192]{2,1,0:T(2,128)(2,1)}, u32[]{:S(2)}, u32[]{:S(2)}) async-start(bf16[8,2,8192]{2,1,0:T(2,128)(2,1)} %reshape.258), calls=%async_computation | async-start | bytes 524288 | tf_op jit(solution)/shard_map/all_to_all | solution.py:137
  87.2 5.9 %all-to-all-done = bf16[8,2,8192]{2,1,0:T(2,128)(2,1)} async-done(((bf16[8,2,8192]{2,1,0:T(2,128)(2,1)}), bf16[8,2,8192]{2,1,0:T(2,128)(2,1)}, u32[]{:S(2)}, u32[]{:S(2)}) %all-to-all-start) | async-done | bytes 262176 | tf_op jit(solution)/shard_map/all_to_all | solution.py:137
  93.1 2.1 reshape.259
  98.8 29.9 %all-reduce.3.cloned.1.call-done = bf16[32,2880]{1,0:T(8,128)(2,1)} async-done(((bf16[32,2880]{1,0:T(8,128)(2,1)}), bf16[32,2880]{1,0:T(8,128)(2,1)}) %all-reduce.3.cloned.1.call-update) | async-done | bytes 184336 | tf_op jit(solution)/shard_map/psum | solution.py:147
  134.3 4.9 %collective-permute-done = f32[32,16]{0,1:T(8,128)S(1)} collective-permute-done((f32[32,16]{0,1:T(8,128)S(1)}, f32[32,16]{0,1:T(8,128)S(1)}, u32[]{:S(2)}, u32[]{:S(2)}) %collective-permute-start) | collective-permute-done | bytes 2080 | tf_op jit(solution)/shard_map/ppermute | solution.py:28
  139.2 4.7 %collective-permute-start.4 = (f32[32,16]{0,1:T(8,128)S(1)}, f32[32,16]{0,1:T(8,128)S(1)}, u32[]{:S(2)}, u32[]{:S(2)}) collective-permute-start(f32[32,16]{0,1:T(8,128)S(1)} %fusion.107), channel_id=1, source_target_pairs={{4,0},{8,4},{12,8},{16,12},{20,16},{24,20},{28,24},{0,28},{5,1},{9... | collective-permute-start | bytes 6152 | tf_op jit(solution)/shard_map/ppermute | solution.py:30
  145.7 4.8 %collective-permute-start.5 = (f32[32,16]{0,1:T(8,128)S(1)}, f32[32,16]{0,1:T(8,128)S(1)}, u32[]{:S(2)}, u32[]{:S(2)}) collective-permute-start(f32[32,16]{0,1:T(8,128)S(1)} %collective-permute-done.4), channel_id=1, source_target_pairs={{4,0},{8,4},{12,8},{16,12},{20,16},{24,20},{28,24},{0,28},{5,1},{9... | collective-permute-start | bytes 6152 | tf_op jit(solution)/shard_map/ppermute | solution.py:30
  152.0 4.9 %collective-permute-start.6 = (f32[32,16]{0,1:T(8,128)S(1)}, f32[32,16]{0,1:T(8,128)S(1)}, u32[]{:S(2)}, u32[]{:S(2)}) collective-permute-start(f32[32,16]{0,1:T(8,128)S(1)} %collective-permute-done.5), channel_id=1, source_target_pairs={{4,0},{8,4},{12,8},{16,12},{20,16},{24,20},{28,24},{0,28},{5,1},{9... | collective-permute-start | bytes 6152 | tf_op jit(solution)/shard_map/ppermute | solution.py:30
  159.1 16.4 %all-gather.2.cloned.1.call-done = bf16[256,2880]{1,0:T(8,128)(2,1)} async-done(((bf16[32,2880]{1,0:T(8,128)(2,1)}), bf16[256,2880]{1,0:T(8,128)(2,1)}) %all-gather.2.cloned.1.call-update) | async-done | bytes 1474576 | tf_op jit(solution)/shard_map/all_gather | solution.py:156
  175.5 5.0 %fusion.48 = f32[256,720]{0,1:T(8,128)} fusion(bf16[256,2880]{1,0:T(8,128)(2,1)} %all-gather.2.cloned.1.call-done, bf16[2,2880,720]{1,2,0:T(8,128)(2,1)} %param.36), kind=kOutput, calls=%fused_computation.39 | convolution fusion | flops 1061867520 | bytes 6483968 | tf_op jit(solution)/shard_map/dot_general | solution.py:164
  180.5 4.4 %fusion.42 = f32[256,720]{0,1:T(8,128)} fusion(bf16[256,2880]{1,0:T(8,128)(2,1)S(1)} %copy-done.13, bf16[2,2880,720]{1,2,0:T(8,128)(2,1)} %param.36), kind=kOutput, calls=%fused_computation.37 | convolution fusion | flops 1061867520 | bytes 6451200 | tf_op jit(solution)/shard_map/dot_general | solution.py:164
  184.9 10.7 %fusion = f32[256,2880]{1,0:T(8,128)} fusion(bf16[2,720,2880]{2,1,0:T(8,128)(2,1)} %param.38, f32[256,720]{0,1:T(8,128)} %fusion.48, bf16[256,2880]{1,0:T(8,128)(2,1)} %all-gather.2.cloned.1.call-done, bf16[2,2880,720]{1,2,0:T(8,128)(2,1)} %param.37, f32[256]{0:T(256)S(1)} %bitcast.221), kind=kOutput, calls=%fused_computation.1 | convolution fusion | flops 2125209600 | bytes 13673472 | tf_op jit(solution)/shard_map/dot_general | solution.py:167
  195.6 11.1 %fusion.21 = bf16[256,2880]{1,0:T(8,128)(2,1)} fusion(f32[256,2880]{1,0:T(8,128)} %fusion, bf16[2,720,2880]{2,1,0:T(8,128)(2,1)} %param.38, f32[256,720]{0,1:T(8,128)} %fusion.42, bf16[256,2880]{1,0:T(8,128)(2,1)} %all-gather.2.cloned.1.call-done, bf16[2,2880,720]{1,2,0:T(8,128)(2,1)} %param.37, f32[256]{0:T(256)S(1)} %bitcast.220), kind=kOutput, calls=%fused_computation.20 | convolution fusion | flops 2126684160 | bytes 15213568 | tf_op jit(solution)/shard_map/dot_general | solution.py:167
  206.7 63.6 %reduce-scatter.2.cloned.1.call-done = bf16[32,2880]{1,0:T(8,128)(2,1)} async-done(((bf16[256,2880]{1,0:T(8,128)(2,1)}), bf16[32,2880]{1,0:T(8,128)(2,1)}) %reduce-scatter.2.cloned.1.call-update) | async-done | bytes 184336 | tf_op jit(solution)/shard_map/reduce_scatter | solution.py:168
  270.4 32.7 %all-reduce.5.cloned.1.call-done = bf16[32,2880]{1,0:T(8,128)(2,1)} async-done(((bf16[32,2880]{1,0:T(8,128)(2,1)}), bf16[32,2880]{1,0:T(8,128)(2,1)}) %all-reduce.5.cloned.1.call-update) | async-done | bytes 184336 | tf_op jit(solution)/shard_map/psum | solution.py:169
  306.1 1.7 fusion.85
  (136 shorter events, 38.6 us)
Async XLA Ops:
  7.2 89.9 %copy-start = (bf16[512,2880]{0,1:T(8,128)(2,1)S(1)}, bf16[512,2880]{0,1:T(8,128)(2,1)}, u32[]{:S(2)}) copy-start(bf16[512,2880]{0,1:T(8,128)(2,1)} %param.33) | copy-start | bytes 8847364
  54.6 5.0 %copy-start.7 = (pred[8,8,4,324]{3,1,2,0:T(8,128)(4,1)}, pred[8,8,4,324]{3,1,2,0:T(8,128)(4,1)S(1)}, u32[]{:S(2)}) copy-start(pred[8,8,4,324]{3,1,2,0:T(8,128)(4,1)S(1)} %pad_add_fusion) | copy-start | bytes 248836
  56.7 11.4 %copy-start.11 = (bf16[4,8,128]{2,1,0:T(8,128)(2,1)S(1)}, bf16[4,8,128]{2,1,0:T(8,128)(2,1)}, u32[]{:S(2)}) copy-start(bf16[4,8,128]{2,1,0:T(8,128)(2,1)} %param.24) | copy-start | bytes 24580
  60.4 12.0 %copy-start.6 = (f32[8,2,8,4,4]{2,4,3,1,0:T(4,128)S(1)}, f32[8,2,8,4,4]{2,4,3,1,0:T(4,128)}, u32[]{:S(2)}) copy-start(f32[8,2,8,4,4]{2,4,3,1,0:T(4,128)} %copy-done.5) | copy-start | bytes 24580
  62.6 16.2 %all-to-all-start.1 = ((f32[8,1,512]{2,1,0:T(1,128)}), f32[8,1,512]{2,1,0:T(1,128)S(1)}, u32[]{:S(2)}, u32[]{:S(2)}) async-start(f32[8,1,512]{2,1,0:T(1,128)} %reshape.260), calls=%async_computation.1 | async-start | bytes 32768 | tf_op jit(solution)/shard_map/all_to_all | solution.py:138
  78.8 14.3 %all-to-all-start = ((bf16[8,2,8192]{2,1,0:T(2,128)(2,1)}), bf16[8,2,8192]{2,1,0:T(2,128)(2,1)}, u32[]{:S(2)}, u32[]{:S(2)}) async-start(bf16[8,2,8192]{2,1,0:T(2,128)(2,1)} %reshape.258), calls=%async_computation | async-start | bytes 524288 | tf_op jit(solution)/shard_map/all_to_all | solution.py:137
  84.8 44.0 %all-reduce.3.cloned.1.call-start = ((), (), s32[]{:S(2)}) async-start(), calls=%async_computation.3 | async-start | bytes 376832 | tf_op jit(solution)/shard_map/psum | solution.py:147
  86.5 42.3 %copy-start.2 = (bf16[4,8,2880]{2,1,0:T(8,128)(2,1)S(1)}, bf16[4,8,2880]{2,1,0:T(8,128)(2,1)}, u32[]{:S(2)}) copy-start(bf16[4,8,2880]{2,1,0:T(8,128)(2,1)} %param.21) | copy-start | bytes 552964
  86.7 43.2 %copy-start.10 = (f32[2880]{0:T(1024)S(1)}, f32[2880]{0:T(1024)}, u32[]{:S(2)}) copy-start(f32[2880]{0:T(1024)} %param.34) | copy-start | bytes 34564
  87.2 44.5 %copy-start.8 = (bf16[2880,16]{0,1:T(8,128)(2,1)S(1)}, bf16[2880,16]{0,1:T(8,128)(2,1)}, u32[]{:S(2)}) copy-start(bf16[2880,16]{0,1:T(8,128)(2,1)} %param.35) | copy-start | bytes 276484
  98.8 76.8 %all-gather.2.cloned.1.call-start = ((), (), s32[]{:S(2)}) async-start(), calls=%async_computation.4 | async-start | bytes 1695744 | tf_op jit(solution)/shard_map/all_gather | solution.py:156
  131.6 138.8 %reduce-scatter.2.cloned.1.call-start = ((), (), s32[]{:S(2)}) async-start(), calls=%async_computation.5 | async-start | bytes 1695744 | tf_op jit(solution)/shard_map/reduce_scatter | solution.py:168
  132.8 6.4 %collective-permute-start = (f32[32,16]{0,1:T(8,128)S(1)}, f32[32,16]{0,1:T(8,128)S(1)}, u32[]{:S(2)}, u32[]{:S(2)}) collective-permute-start(f32[32,16]{0,1:T(8,128)S(1)} %fusion.107), channel_id=1, source_target_pairs={{0,4},{4,8},{8,12},{12,16},{16,20},{20,24},{24,28},{28,0},{1,5},{5... | collective-permute-start | bytes 6152 | tf_op jit(solution)/shard_map/ppermute | solution.py:28
  139.2 6.4 %collective-permute-start.1 = (f32[32,16]{0,1:T(8,128)S(1)}, f32[32,16]{0,1:T(8,128)S(1)}, u32[]{:S(2)}, u32[]{:S(2)}) collective-permute-start(f32[32,16]{0,1:T(8,128)S(1)} %collective-permute-done), channel_id=1, source_target_pairs={{0,4},{4,8},{8,12},{12,16},{16,20},{20,24},{24,28},{28,0},{1,5},{5... | collective-permute-start | bytes 6152 | tf_op jit(solution)/shard_map/ppermute | solution.py:28
  139.2 6.5 %collective-permute-start.4 = (f32[32,16]{0,1:T(8,128)S(1)}, f32[32,16]{0,1:T(8,128)S(1)}, u32[]{:S(2)}, u32[]{:S(2)}) collective-permute-start(f32[32,16]{0,1:T(8,128)S(1)} %fusion.107), channel_id=1, source_target_pairs={{4,0},{8,4},{12,8},{16,12},{20,16},{24,20},{28,24},{0,28},{5,1},{9... | collective-permute-start | bytes 6152 | tf_op jit(solution)/shard_map/ppermute | solution.py:30
  145.7 6.3 %collective-permute-start.2 = (f32[32,16]{0,1:T(8,128)S(1)}, f32[32,16]{0,1:T(8,128)S(1)}, u32[]{:S(2)}, u32[]{:S(2)}) collective-permute-start(f32[32,16]{0,1:T(8,128)S(1)} %collective-permute-done.1), channel_id=1, source_target_pairs={{0,4},{4,8},{8,12},{12,16},{16,20},{20,24},{24,28},{28,0},{1,5},{5... | collective-permute-start | bytes 6152 | tf_op jit(solution)/shard_map/ppermute | solution.py:28
  145.7 6.3 %collective-permute-start.5 = (f32[32,16]{0,1:T(8,128)S(1)}, f32[32,16]{0,1:T(8,128)S(1)}, u32[]{:S(2)}, u32[]{:S(2)}) collective-permute-start(f32[32,16]{0,1:T(8,128)S(1)} %collective-permute-done.4), channel_id=1, source_target_pairs={{4,0},{8,4},{12,8},{16,12},{20,16},{24,20},{28,24},{0,28},{5,1},{9... | collective-permute-start | bytes 6152 | tf_op jit(solution)/shard_map/ppermute | solution.py:30
  152.0 6.3 %collective-permute-start.3 = (f32[32,16]{0,1:T(8,128)S(1)}, f32[32,16]{0,1:T(8,128)S(1)}, u32[]{:S(2)}, u32[]{:S(2)}) collective-permute-start(f32[32,16]{0,1:T(8,128)S(1)} %collective-permute-done.2), channel_id=1, source_target_pairs={{0,4},{4,8},{8,12},{12,16},{16,20},{20,24},{24,28},{28,0},{1,5},{5... | collective-permute-start | bytes 6152 | tf_op jit(solution)/shard_map/ppermute | solution.py:28
  152.0 6.4 %collective-permute-start.6 = (f32[32,16]{0,1:T(8,128)S(1)}, f32[32,16]{0,1:T(8,128)S(1)}, u32[]{:S(2)}, u32[]{:S(2)}) collective-permute-start(f32[32,16]{0,1:T(8,128)S(1)} %collective-permute-done.5), channel_id=1, source_target_pairs={{4,0},{8,4},{12,8},{16,12},{20,16},{24,20},{28,24},{0,28},{5,1},{9... | collective-permute-start | bytes 6152 | tf_op jit(solution)/shard_map/ppermute | solution.py:30
  175.5 5.0 %copy-start.13 = (bf16[256,2880]{1,0:T(8,128)(2,1)S(1)}, bf16[256,2880]{1,0:T(8,128)(2,1)}, u32[]{:S(2)}) copy-start(bf16[256,2880]{1,0:T(8,128)(2,1)} %all-gather.2.cloned.1.call-done) | copy-start | bytes 4423684
  195.6 107.5 %copy-start.3 = (bf16[32,2880]{1,0:T(8,128)(2,1)S(1)}, bf16[32,2880]{1,0:T(8,128)(2,1)}, u32[]{:S(2)}) copy-start(bf16[32,2880]{1,0:T(8,128)(2,1)} %all-reduce.3.cloned.1.call-done) | copy-start | bytes 552964
  195.6 108.8 %copy-start.9 = (f32[2880]{0:T(1024)S(1)}, f32[2880]{0:T(1024)}, u32[]{:S(2)}) copy-start(f32[2880]{0:T(1024)} %param.39) | copy-start | bytes 34564
  206.7 96.4 %all-reduce.5.cloned.1.call-start = ((), (), s32[]{:S(2)}) async-start(), calls=%async_computation.6 | async-start | bytes 376832 | tf_op jit(solution)/shard_map/psum | solution.py:169
  303.0 4.8 %copy-start.4 = (bf16[2880,512]{1,0:T(8,128)(2,1)S(1)}, bf16[2880,512]{1,0:T(8,128)(2,1)}, u32[]{:S(2)}) copy-start(bf16[2880,512]{1,0:T(8,128)(2,1)} %param.40) | copy-start | bytes 8847364
  (4 other events, 12.5 us)
Sparse Core Ops, SparseCore 0:
  98.9 29.8 all-reduce.2
  131.7 43.7 all-gather.1
  206.8 63.5 reduce-scatter.1
  272.5 30.4 all-reduce.4
